TPU v7x, 32 devices: a whole 2x2x4 slice. The times are simulated.
32 devices in a mesh: lat: 4 (over y, x), ord: 8 (over z, core).
Axes of the slice: x: 2, y: 2, z: 4, core: 2. Of those that a mesh axis runs over, the one named last changes fastest.
Arguments:
- field: bfloat16 [32, 64, 256], P(('lat', 'ord')), may hold values from -6 to 6
- tap_mask: int32 [32, 8, 15], P(('lat', 'ord')), may hold values 0 or 1
- tap_weight: float32 [32, 8, 15], P(('lat', 'ord')), may hold values from -1.4 to 1.4
- basis_mix: bfloat16 [8, 256, 256], replicated, may hold values from -0.125 to 0.125
- order_slots: int32 [32], replicated, may hold values from 0 to 31, each once
- degree_gain: float32 [32, 256], replicated, may hold values from 0.3 to 3
- spectral_mix: bfloat16 [2, 256, 256], replicated, may hold values from -0.25 to 0.25
Outputs:
- spectrum: bfloat16 [32, 32, 2, 256], P('lat', 'ord')
Inputs may be any that keep to these rules, and one draw needn't show every extreme that they name: `order_slots`: each order 0 to 31 stands in exactly one slot.
All inputs are finite; a program needn't handle non-finite values. No bound on the sum of `tap_mask` on one device may be relied on, other than what follows from the above.
Results may differ from a plain program's by a relative error of at most 0.0095.
Values may be sent and summed in bfloat16 or wider, within the bound.
A program may use at most 64 MiB of HBM per device.

v0:
```python
import math

import jax
import jax.numpy as jnp
from jax import lax
from jax.sharding import PartitionSpec as P


def extended(block, sides, width):
    for axis, dim in sides:
        count = lax.axis_size(axis)
        forward = [(i, i + 1) for i in range(count - 1)]
        backward = [(target, source) for source, target in forward]
        low = lax.ppermute(
            lax.slice_in_dim(block, block.shape[dim] - width, None, axis=dim), axis, forward
        )
        high = lax.ppermute(lax.slice_in_dim(block, 0, width, axis=dim), axis, backward)
        block = jnp.concatenate([low, block, high], axis=dim)
    return block


def fourier_table(order_slots, n_lon):
    points = jnp.arange(n_lon, dtype=jnp.int32)
    phase_int = order_slots[:, None] * points[None, :] % n_lon
    angles = phase_int.astype(jnp.float32) * (2.0 * math.pi / n_lon)
    factor = 1.0 / math.sqrt(n_lon)
    stacked = jnp.stack([jnp.cos(angles) * factor, -jnp.sin(angles) * factor], axis=1)
    return stacked.reshape(2 * order_slots.shape[0], n_lon).astype(jnp.bfloat16)


def latitude_table(orders, wavenumbers, lat_rows, n_lat):
    phase_int = wavenumbers[None, :, None] * (2 * lat_rows[None, None, :] + 1) % (4 * n_lat)
    angles = phase_int.astype(jnp.float32) * (math.pi / (2 * n_lat))
    factor = math.sqrt(2.0 / n_lat)
    is_even = (orders % 2 == 0)[:, None, None]
    return (jnp.where(is_even, jnp.cos(angles), jnp.sin(angles)) * factor).astype(jnp.bfloat16)


def disco(lat_rows, filters, out_rows):
    running = None
    for lat_step in range(3):
        cycle_rows = lat_rows[lat_step : lat_step + out_rows].astype(jnp.float32)
        for lon_step in range(5):
            shifted = jnp.roll(cycle_rows, 2 - lon_step, axis=1)
            tap_vals = filters[:, :, 5 * lat_step + lon_step]
            tap_term = tap_vals[:, None, :, None] * shifted[:, :, None, :]
            running = tap_term if running is None else running + tap_term
    return running.astype(jnp.bfloat16)


def mixing(spectral_mix):
    real_part = spectral_mix[0]
    imag_part = spectral_mix[1]
    top_rows = jnp.concatenate([real_part, imag_part], axis=1)
    bottom_rows = jnp.concatenate([-imag_part, real_part], axis=1)
    return jnp.concatenate([top_rows, bottom_rows], axis=0)


def per_device(field, tap_mask, tap_weight, basis_mix, order_slots, degree_gain, spectral_mix):
    rows_here, n_lon, channels = field.shape
    basis_count = basis_mix.shape[0]
    n_lat = degree_gain.shape[0]
    n_orders = order_slots.shape[0]
    filters = tap_mask.astype(jnp.float32) * tap_weight
    padded = extended(field, ((("lat", "ord"), 0),), 1)
    tap_sums = disco(padded, filters, rows_here)
    grid_rows = jnp.dot(
        tap_sums.reshape(rows_here * n_lon, basis_count * channels),
        basis_mix.reshape(basis_count * channels, channels),
        preferred_element_type=jnp.float32,
    ).astype(jnp.bfloat16)
    grid_rows = grid_rows.reshape(rows_here, n_lon, channels)
    dft_table = fourier_table(order_slots, n_lon)
    spectra = jnp.einsum("fj,rjc->rfc", dft_table, grid_rows, preferred_element_type=jnp.float32)
    fourier = spectra.astype(jnp.bfloat16).reshape(rows_here, n_orders, 2, channels)
    by_orders = lax.all_to_all(fourier, "ord", split_axis=1, concat_axis=0, tiled=True)
    slot_count = by_orders.shape[1]
    my_orders = lax.dynamic_slice_in_dim(
        order_slots, lax.axis_index("ord") * slot_count, slot_count
    )
    mix_matrix = mixing(spectral_mix)
    waves_here = n_lat // lax.axis_size("lat")
    first_wave = lax.axis_index("lat") * waves_here
    wavenumbers = first_wave + jnp.arange(waves_here, dtype=jnp.int32)
    portion = lax.all_gather(by_orders, "lat", axis=0, tiled=True)
    number = portion.shape[0]
    lat_rows = jnp.arange(number, dtype=jnp.int32)
    lat_basis = latitude_table(my_orders, wavenumbers, lat_rows, n_lat)
    flat_rows = portion.reshape(number, slot_count, 2 * channels)
    coefficients = jnp.einsum(
        "ski,isx->ksx", lat_basis, flat_rows, preferred_element_type=jnp.float32
    )
    gain_rows = lax.dynamic_slice_in_dim(degree_gain, first_wave, waves_here, 0)
    scaled = (
        coefficients.reshape(waves_here, slot_count, 2, channels) * gain_rows[:, None, None, :]
    ).astype(jnp.bfloat16)
    mixed_rows = jnp.dot(
        scaled.reshape(waves_here * slot_count, 2 * channels),
        mix_matrix,
        preferred_element_type=jnp.float32,
    ).astype(jnp.bfloat16)
    return mixed_rows.reshape(waves_here, slot_count, 2, channels)


def solution(mesh):
    in_specs = (
        P(("lat", "ord"), None, None),
        P(("lat", "ord"), None, None),
        P(("lat", "ord"), None, None),
        P(),
        P(),
        P(),
        P(),
    )
    out_specs = P("lat", "ord", None, None)
    return jax.shard_map(
        per_device, mesh=mesh, in_specs=in_specs, out_specs=out_specs, check_vma=False
    )
```

profile of v0, /device:TPU:0, one launch (start us, length us, event | category | flops | bytes accessed | tf_op | source)
XLA Modules:
  0.0 37.1 jit_solution(447096436004004995)
XLA Ops:
  0.0 1.4 %collective-permute-start.1 = (bf16[1,64,256]{2,1,0:T(8,128)(2,1)}, bf16[1,64,256]{2,1,0:T(8,128)(2,1)S(1)}, u32[]{:S(2)}, u32[]{:S(2)}) collective-permute-start(bf16[1,64,256]{2,1,0:T(8,128)(2,1)} %param.7), channel_id=1, source_target_pairs={{1,0},{2,1},{3,2},{4,3},{5,4},{6,5},{7,6},{8,7},{9,8},{10,9},{11,1... | collective-permute-start | bytes 98312 | tf_op jit(solution)/shard_map/ppermute | solution.py:17
  1.4 3.0 %collective-permute-start = (bf16[1,64,256]{2,1,0:T(8,128)(2,1)}, bf16[1,64,256]{2,1,0:T(8,128)(2,1)S(1)}, u32[]{:S(2)}, u32[]{:S(2)}) collective-permute-start(bf16[1,64,256]{2,1,0:T(8,128)(2,1)} %param.7), channel_id=1, source_target_pairs={{0,1},{1,2},{2,3},{3,4},{4,5},{5,6},{6,7},{7,8},{8,9},{9,10},{10,1... | collective-permute-start | bytes 98312 | tf_op jit(solution)/shard_map/ppermute | solution.py:14
  4.5 0.8 %fusion.94 = (f32[1,62,256]{2,1,0:T(8,128)S(1)}, f32[1,62,256]{2,1,0:T(8,128)S(1)}) fusion(bf16[1,64,256]{2,1,0:T(8,128)(2,1)} %param.7), kind=kLoop, calls=%fused_computation.121 | loop fusion | bytes 253952 | tf_op jit(solution)/shard_map/jit(_roll_static)/slice | solution.py:44
  5.4 0.0 copy-start.3
  5.4 0.0 copy-start.4
  5.5 0.6 %copy-done.3 = f32[1,8,15]{2,1,0:T(8,128)S(1)} copy-done((f32[1,8,15]{2,1,0:T(8,128)S(1)}, f32[1,8,15]{2,1,0:T(8,128)}, u32[]{:S(2)}) %copy-start.3) | copy-done | bytes 504
  6.1 0.0 copy-done.4
  6.1 0.4 %slice_reduce_fusion.14 = (f32[8]{0:T(128)S(1)}, f32[8]{0:T(128)S(1)}, f32[8]{0:T(128)S(1)}, f32[8]{0:T(128)S(1)}, f32[8]{0:T(128)S(1)}, /*index=5*/f32[8]{0:T(1...) fusion(f32[1,8,15]{2,1,0:T(8,128)S(1)} %convert_multiply_fusion), kind=kLoop, calls=%fused_computation.101 | loop fusion | bytes 960 | tf_op jit(solution)/shard_map/slice | solution.py:45
  6.5 0.3 copy-done.5
  6.8 0.2 multiply_convert_fusion.4
  7.0 0.1 fusion.83
  7.2 0.7 %constant_dynamic-slice_fusion = f32[8,256]{1,0:T(8,128)S(1)} fusion(f32[32,256]{1,0:T(8,128)} %param.12, s32[]{:T(128)S(6)} %select_n.53), kind=kLoop, calls=%fused_computation.112 | loop fusion | bytes 16388 | tf_op jit(solution)/shard_map/dynamic_slice | solution.py:93
  7.9 0.0 collective-permute-done.1
  8.0 0.0 collective-permute-done
  8.2 0.8 %fusion.1 = bf16[1,64,256]{2,1,0:T(8,128)(2,1)S(1)} fusion(bf16[64,64]{1,0:T(8,128)(2,1)S(1)} %bitcast.62, bf16[8,256,256]{2,1,0:T(8,128)(2,1)S(1)} %copy-done, f32[64,256]{1,0:T(8,128)S(1)} %get-tuple-element.51, f32[8]{0:T(128)S(1)} %get-tuple-element.6, f32[64,256]{1,0:T(8,128)S(1)} %get-tuple-element.53, f32[8]{0:T(128)S(1)} %get-tuple-element.7, ...), kind=kOutput, calls=%fused_computation.5 | convolution fusion | flops 73170944 | bytes 2073056 | tf_op jit(solution)/shard_map/fj,rjc->rfc/dot_general | solution.py:74
  9.0 0.7 %reshape.451 = bf16[1,32,2,256]{3,2,1,0:T(2,128)(2,1)} reshape(bf16[1,64,256]{2,1,0:T(8,128)(2,1)S(1)} %fusion.1) | data formatting | bytes 65536 | tf_op jit(solution)/shard_map/reshape | solution.py:75
  9.7 9.7 %all-to-all-start = ((bf16[1,32,2,256]{3,2,0,1:T(2,128)(2,1)}), bf16[1,32,2,256]{3,2,0,1:T(2,128)(2,1)S(1)}, u32[]{:S(2)}, u32[]{:S(2)}) async-start(bf16[1,32,2,256]{3,2,0,1:T(2,128)(2,1)} %bitcast.19), calls=%async_computation | async-start | bytes 65536 | tf_op jit(solution)/shard_map/all_to_all | solution.py:76
  19.4 0.1 fusion.84
  19.5 5.7 %all-to-all-done = bf16[1,32,2,256]{3,2,0,1:T(2,128)(2,1)S(1)} async-done(((bf16[1,32,2,256]{3,2,0,1:T(2,128)(2,1)}), bf16[1,32,2,256]{3,2,0,1:T(2,128)(2,1)S(1)}, u32[]{:S(2)}, u32[]{:S(2)}) %all-to-all-start) | async-done | bytes 32800 | tf_op jit(solution)/shard_map/all_to_all | solution.py:76
  25.1 10.7 %all_gather.3 = bf16[32,4,2,256]{3,2,0,1:T(2,128)(2,1)S(1)} all-gather(bf16[8,4,2,256]{3,2,0,1:T(2,128)(2,1)S(1)} %copy.19), channel_id=1, replica_groups=mesh['lat'=4,'ord'=8] {'lat'}, dimensions={0}, use_global_device_ids=true | all-gather | bytes 163840 | tf_op jit(solution)/shard_map/all_gather | solution.py:85
  35.9 0.1 reshape.452
  35.9 0.2 convolution_bitcast_fusion
  36.2 0.2 convolution_convert_fusion.1
  36.4 0.6 %reshape.454 = bf16[8,4,2,256]{3,2,1,0:T(2,128)(2,1)} reshape(bf16[32,512]{1,0:T(8,128)(2,1)S(1)} %convolution_convert_fusion.1) | data formatting | bytes 65536 | tf_op jit(solution)/shard_map/reshape | solution.py:102
  (39 shorter events, 0.4 us)
Async XLA Ops:
  0.0 8.2 %copy-start = (bf16[8,256,256]{2,1,0:T(8,128)(2,1)S(1)}, bf16[8,256,256]{2,1,0:T(8,128)(2,1)}, u32[]{:S(2)}) copy-start(bf16[8,256,256]{2,1,0:T(8,128)(2,1)} %param.10) | copy-start | bytes 3145732
  0.0 5.3 %copy-start.1 = (bf16[1,64,256]{2,1,0:T(8,128)(2,1)S(1)}, bf16[1,64,256]{2,1,0:T(8,128)(2,1)}, u32[]{:S(2)}) copy-start(bf16[1,64,256]{2,1,0:T(8,128)(2,1)} %param.7) | copy-start | bytes 98308
  0.0 5.4 %copy-start.2 = (bf16[2,256,256]{2,1,0:T(8,128)(2,1)S(1)}, bf16[2,256,256]{2,1,0:T(8,128)(2,1)}, u32[]{:S(2)}) copy-start(bf16[2,256,256]{2,1,0:T(8,128)(2,1)} %param.13) | copy-start | bytes 786436
  0.0 7.9 %collective-permute-start.1 = (bf16[1,64,256]{2,1,0:T(8,128)(2,1)}, bf16[1,64,256]{2,1,0:T(8,128)(2,1)S(1)}, u32[]{:S(2)}, u32[]{:S(2)}) collective-permute-start(bf16[1,64,256]{2,1,0:T(8,128)(2,1)} %param.7), channel_id=1, source_target_pairs={{1,0},{2,1},{3,2},{4,3},{5,4},{6,5},{7,6},{8,7},{9,8},{10,9},{11,1... | collective-permute-start | bytes 98312 | tf_op jit(solution)/shard_map/ppermute | solution.py:17
  1.4 6.6 %collective-permute-start = (bf16[1,64,256]{2,1,0:T(8,128)(2,1)}, bf16[1,64,256]{2,1,0:T(8,128)(2,1)S(1)}, u32[]{:S(2)}, u32[]{:S(2)}) collective-permute-start(bf16[1,64,256]{2,1,0:T(8,128)(2,1)} %param.7), channel_id=1, source_target_pairs={{0,1},{1,2},{2,3},{3,4},{4,5},{5,6},{6,7},{7,8},{8,9},{9,10},{10,1... | collective-permute-start | bytes 98312 | tf_op jit(solution)/shard_map/ppermute | solution.py:14
  5.4 0.7 %copy-start.3 = (f32[1,8,15]{2,1,0:T(8,128)S(1)}, f32[1,8,15]{2,1,0:T(8,128)}, u32[]{:S(2)}) copy-start(f32[1,8,15]{2,1,0:T(8,128)} %param.9) | copy-start | bytes 1444
  5.4 0.7 %copy-start.4 = (s32[1,8,15]{2,1,0:T(8,128)S(1)}, s32[1,8,15]{2,1,0:T(8,128)}, u32[]{:S(2)}) copy-start(s32[1,8,15]{2,1,0:T(8,128)} %param.8) | copy-start | bytes 1444
  6.1 0.7 %copy-start.5 = (s32[32]{0:T(128)S(1)}, s32[32]{0:T(128)}, u32[]{:S(2)}) copy-start(s32[32]{0:T(128)} %param.11) | copy-start | bytes 388
  9.7 15.4 %all-to-all-start = ((bf16[1,32,2,256]{3,2,0,1:T(2,128)(2,1)}), bf16[1,32,2,256]{3,2,0,1:T(2,128)(2,1)S(1)}, u32[]{:S(2)}, u32[]{:S(2)}) async-start(bf16[1,32,2,256]{3,2,0,1:T(2,128)(2,1)} %bitcast.19), calls=%async_computation | async-start | bytes 65536 | tf_op jit(solution)/shard_map/all_to_all | solution.py:76
where the time goes:
time: 37.4 us; the launch traced here: 37.1 us
  starting transfers between devices  14.1 us (38%)
  blocking collectives  10.7 us (29%)
  waiting for transfers between devices  5.66 us (15%)
  local copies, waits for them, and re-layouts  4.54 us (12%)
  matrix products  1.2 us (3%)
  other arithmetic  0.49 us (1%)
    all_gather x1, blocking collectives, per_device(): portion = lax.all_gather(by_orders, 'lat', axis=0, tiled=True)  10.7 us
    all_to_all x1, starting transfers between devices, per_device(): lax.all_to_all(fourier, 'ord', split_axis=1, concat_axis=0, tiled=True)  9.69 us
    all_to_all x1, waiting for transfers between devices, per_device(): lax.all_to_all(fourier, 'ord', split_axis=1, concat_axis=0, tiled=True)  5.66 us
    ppermute x1, starting transfers between devices, extended(): lax.ppermute(lax.slice_in_dim(block, block.shape[dim] - width, None, axis...  3.03 us
    ppermute x1, starting transfers between devices, extended(): lax.ppermute(lax.slice_in_dim(block, 0, width, axis=dim), axis, backward)  1.41 us
    unnamed x13, local copies, waits for them, and re-layouts  0.95 us
    slice x12, local copies, waits for them, and re-layouts, disco(): shifted = jnp.roll(cycle_rows, 2 - lon_step, axis=1)  0.94 us
    dot_general x1, matrix products, per_device(): jnp.einsum('fj,rjc->rfc', dft_table, grid_rows, preferred_element_type=jn...  0.82 us
  transfers between devices with their start and end apart: 3, of which 1 were waited for; matrix products, arithmetic and copies ran while one was open for 7% of the time, Pallas kernels for 0%

commit v1 on v0

v1 whole, which is shorter than its diff:
```python
import functools
import math

import jax
import jax.numpy as jnp
from jax import lax
from jax.experimental import pallas as pl
from jax.experimental.pallas import tpu as pltpu
from jax.sharding import PartitionSpec as P

MESH = pl.DeviceIdType.MESH
F32 = jnp.float32
BF16 = jnp.bfloat16
PAD = 8
SLAB = 8


def log2(n):
    assert n & (n - 1) == 0
    return n.bit_length() - 1


def cosine(phase_int, period):
    q = phase_int & (period - 1)
    r = jnp.minimum(q, period - q)
    x = (period // 4 - r).astype(F32) * (2.0 * math.pi / period)
    x2 = x * x
    total = jnp.full_like(x, -1.0 / math.factorial(11))
    for power, sign in ((9, 1.0), (7, -1.0), (5, 1.0), (3, -1.0), (1, 1.0)):
        total = total * x2 + sign / math.factorial(power)
    return total * x


def iota(shape, dim):
    return lax.broadcasted_iota(jnp.int32, shape, dim)


def repeat(count, body):
    if count == 1:
        body(0)
    else:
        pl.loop(0, count)(body)


def kernel(
    dims,
    mask_ref, weight_ref, slots_ref, field_hbm, basis_hbm, gain_hbm, spectral_hbm,
    out_ref,
    rows_in, padded, taps, basis, gain, spectral, grid, table, sent, held, lat_mat,
    local_sem, halo_send, halo_recv, ord_send, ord_recv, lat_send, lat_recv,
):
    n_lat_dev, n_ord_dev, n_lat, n_lon, n_orders, channels, basis_count = dims
    lat_id = lax.axis_index("lat")
    ord_id = lax.axis_index("ord")
    row_id = lat_id * n_ord_dev + ord_id
    slots_here = n_orders // n_ord_dev
    waves = n_lat // n_lat_dev
    per_slab = min(SLAB // 2, slots_here)
    width = 2 * per_slab
    groups = slots_here // per_slab
    has_prev = row_id > 0
    has_next = row_id < n_lat - 1
    prev_dev = ((row_id - 1) // n_ord_dev, (row_id - 1) % n_ord_dev)
    next_dev = ((row_id + 1) // n_ord_dev, (row_id + 1) % n_ord_dev)
    far_prev = jnp.logical_and(ord_id == 0, has_prev)
    far_next = jnp.logical_and(ord_id == n_ord_dev - 1, has_next)

    barrier = pltpu.get_barrier_semaphore()

    @pl.when(far_prev)
    def _():
        pl.semaphore_signal(barrier, inc=1, device_id=prev_dev, device_id_type=MESH)

    @pl.when(far_next)
    def _():
        pl.semaphore_signal(barrier, inc=1, device_id=next_dev, device_id_type=MESH)

    for step in range(1, n_ord_dev):
        pl.semaphore_signal(
            barrier, inc=1, device_id=(lat_id, lax.rem(ord_id + step, n_ord_dev)), device_id_type=MESH
        )
    for step in range(1, n_lat_dev):
        pl.semaphore_signal(
            barrier, inc=1, device_id=(lax.rem(lat_id + step, n_lat_dev), ord_id), device_id_type=MESH
        )

    own_copy = pltpu.make_async_copy(field_hbm, rows_in.at[pl.ds(1, 1)], local_sem.at[0])
    basis_copy = pltpu.make_async_copy(basis_hbm, basis, local_sem.at[1])
    gain_copy = pltpu.make_async_copy(
        gain_hbm.at[pl.ds(pl.multiple_of(lat_id * waves, waves), waves)], gain, local_sem.at[2]
    )
    spectral_copy = pltpu.make_async_copy(spectral_hbm, spectral, local_sem.at[3])
    own_copy.start()
    basis_copy.start()
    gain_copy.start()
    spectral_copy.start()

    @pl.when(jnp.logical_not(has_prev))
    def _():
        rows_in[0] = jnp.zeros(rows_in.shape[1:], BF16)

    @pl.when(jnp.logical_not(has_next))
    def _():
        rows_in[2] = jnp.zeros(rows_in.shape[1:], BF16)

    orders = slots_ref[...]

    def pick(slot_of_row):
        found = iota((slot_of_row.shape[0], n_orders), 1) == slot_of_row
        return jnp.sum(jnp.where(found, orders.astype(F32), 0.0), axis=1, keepdims=True).astype(jnp.int32)

    block_rows = table.shape[0]

    def dft_block(start):
        row = iota((block_rows, 1), 0) + start
        order = pick(row >> 1)
        phase = order * iota((block_rows, n_lon), 1) + (n_lon // 4) * (row & 1)
        table[...] = (cosine(phase, n_lon) * (1.0 / math.sqrt(n_lon))).astype(BF16)

    lat_rows = min(n_lat, 256 // width)
    out_rows = waves * width

    def lat_block(group, part):
        row = iota((out_rows, 1), 0)
        col = iota((1, lat_rows * width), 1)
        wave = (row >> log2(width)) + lat_id * waves
        slot = (row & (width - 1)) >> 1
        order = pick(slot + ord_id * slots_here + group * per_slab)
        lat = (col >> log2(width)) + part * lat_rows
        phase = wave * (2 * lat + 1) + jnp.where((order & 1) == 0, 0, 3 * n_lat)
        value = cosine(phase, 4 * n_lat) * math.sqrt(2.0 / n_lat)
        apart = (row & (width - 1)) ^ (col & (width - 1))
        straight = jnp.where(apart == 0, value, 0.0)
        turned = jnp.where(apart == 1, jnp.where((row & 1) == 0, -value, value), 0.0)
        lat_mat[:out_rows] = straight.astype(BF16)
        lat_mat[out_rows:] = turned.astype(BF16)

    single_dft = block_rows == 2 * n_orders
    single_lat = groups == 1 and lat_rows == n_lat
    if single_dft:
        dft_block(0)

    others = (n_ord_dev - 1) + (n_lat_dev - 1)
    pl.semaphore_wait(barrier, others + far_prev.astype(jnp.int32) + far_next.astype(jnp.int32))

    to_next = pltpu.make_async_remote_copy(
        src_ref=field_hbm, dst_ref=rows_in.at[pl.ds(0, 1)], send_sem=halo_send.at[0],
        recv_sem=halo_recv.at[0], device_id=next_dev, device_id_type=MESH,
    )
    to_prev = pltpu.make_async_remote_copy(
        src_ref=field_hbm, dst_ref=rows_in.at[pl.ds(2, 1)], send_sem=halo_send.at[1],
        recv_sem=halo_recv.at[1], device_id=prev_dev, device_id_type=MESH,
    )
    pl.when(has_next)(to_next.start)
    pl.when(has_prev)(to_prev.start)
    if single_lat:
        lat_block(0, 0)

    def spread(which):
        row = rows_in[which].astype(F32)
        padded[which, pl.ds(PAD, n_lon)] = row
        padded[which, pl.ds(0, PAD)] = row[n_lon - PAD:]
        padded[which, pl.ds(PAD + n_lon, PAD)] = row[:PAD]

    own_copy.wait()
    spread(1)
    pl.when(has_prev)(to_next.wait_recv)
    spread(0)
    pl.when(has_next)(to_prev.wait_recv)
    spread(2)

    lon_block = min(n_lon, 64)
    lon_piece = 16
    basis_copy.wait()

    def convolve(block):
        for piece in range(lon_block // lon_piece):
            offset = piece * lon_piece
            first = offset if isinstance(block, int) else pl.multiple_of(block * lon_block, lon_block) + offset
            if isinstance(block, int):
                window = padded[:, first: first + lon_piece + 2 * PAD]
            else:
                window = padded[:, pl.ds(first, lon_piece + 2 * PAD)]
            shifted = [
                window[lat_step, PAD + lon_step - 2: PAD + lon_step - 2 + lon_piece]
                for lat_step in range(3)
                for lon_step in range(5)
            ]
            for b in range(basis_count):
                total = None
                for tap in range(15):
                    term = (mask_ref[0, b, tap].astype(F32) * weight_ref[0, b, tap]) * shifted[tap]
                    total = term if total is None else total + term
                taps[pl.ds(offset, lon_piece), pl.ds(b * channels, channels)] = total.astype(BF16)
        mixed = jnp.dot(
            taps[...], basis[...].reshape(basis_count * channels, channels), preferred_element_type=F32
        )
        start = block * lon_block if isinstance(block, int) else pl.multiple_of(block * lon_block, lon_block)
        grid[pl.ds(start, lon_block)] = mixed.astype(BF16)

    repeat(n_lon // lon_block, convolve)

    slabs = block_rows // width

    def transform(block):
        if not single_dft:
            dft_block(block * block_rows)
        rows = jnp.dot(table[...], grid[...], preferred_element_type=F32).astype(BF16)
        sent[pl.ds(block * slabs, slabs)] = rows.reshape(slabs, width, channels)

    repeat(2 * n_orders // block_rows, transform)

    def ord_copy(step):
        peer = lax.rem(ord_id + step, n_ord_dev)
        return pltpu.make_async_remote_copy(
            src_ref=sent.at[pl.ds(peer * groups, groups)], dst_ref=held.at[:, row_id],
            send_sem=ord_send.at[step], recv_sem=ord_recv.at[step],
            device_id=(lat_id, peer), device_id_type=MESH,
        )

    def ord_arrival(step):
        source = lat_id * n_ord_dev + lax.rem(ord_id + n_ord_dev - step, n_ord_dev)
        return pltpu.make_async_remote_copy(
            src_ref=sent.at[pl.ds(0, groups)], dst_ref=held.at[:, source],
            send_sem=ord_send.at[step], recv_sem=ord_recv.at[step],
            device_id=(lat_id, ord_id), device_id_type=MESH,
        )

    for step in range(1, n_ord_dev):
        ord_copy(step).start()
    held[:, row_id] = sent[pl.ds(ord_id * groups, groups)]
    for step in range(1, n_ord_dev):
        ord_arrival(step).wait_recv()

    def lat_copy(step):
        band = pl.ds(lat_id * n_ord_dev, n_ord_dev)
        return pltpu.make_async_remote_copy(
            src_ref=held.at[:, band], dst_ref=held.at[:, band],
            send_sem=lat_send.at[step], recv_sem=lat_recv.at[step],
            device_id=(lax.rem(lat_id + step, n_lat_dev), ord_id), device_id_type=MESH,
        )

    def lat_arrival(step):
        source = lax.rem(lat_id + n_lat_dev - step, n_lat_dev)
        band = pl.ds(source * n_ord_dev, n_ord_dev)
        return pltpu.make_async_remote_copy(
            src_ref=held.at[:, band], dst_ref=held.at[:, band],
            send_sem=lat_send.at[step], recv_sem=lat_recv.at[step],
            device_id=(lat_id, ord_id), device_id_type=MESH,
        )

    for step in range(1, n_lat_dev):
        lat_copy(step).start()
    pl.when(has_next)(to_next.wait_send)
    pl.when(has_prev)(to_prev.wait_send)
    for step in range(1, n_ord_dev):
        ord_copy(step).wait_send()
    gain_copy.wait()
    spectral_copy.wait()
    for step in range(1, n_lat_dev):
        lat_arrival(step).wait_recv()

    def latitude(group, part):
        rows = held[group, pl.ds(part * lat_rows, lat_rows)].reshape(lat_rows * width, channels)
        return jnp.dot(lat_mat[...], rows, preferred_element_type=F32)

    def finish(group):
        if single_lat:
            total = latitude(group, 0)
        else:
            def add(part, so_far):
                lat_block(group, part)
                return so_far + latitude(group, part)

            total = lax.fori_loop(
                0, n_lat // lat_rows, add, jnp.zeros((2 * out_rows, channels), F32)
            )
        gains = jnp.broadcast_to(gain[...][:, None, :], (waves, width, channels)).reshape(out_rows, channels)
        straight = (total[:out_rows] * gains).astype(BF16)
        turned = (total[out_rows:] * gains).astype(BF16)
        result = jnp.dot(straight, spectral[0], preferred_element_type=F32) + jnp.dot(
            turned, spectral[1], preferred_element_type=F32
        )
        out_ref[group] = result.astype(BF16)

    repeat(groups, finish)
    for step in range(1, n_lat_dev):
        lat_copy(step).wait_send()


def per_device(field, tap_mask, tap_weight, basis_mix, order_slots, degree_gain, spectral_mix):
    rows_here, n_lon, channels = field.shape
    assert rows_here == 1
    basis_count = basis_mix.shape[0]
    n_lat = degree_gain.shape[0]
    n_orders = order_slots.shape[0]
    n_lat_dev = lax.axis_size("lat")
    n_ord_dev = lax.axis_size("ord")
    slots_here = n_orders // n_ord_dev
    waves = n_lat // n_lat_dev
    per_slab = min(SLAB // 2, slots_here)
    width = 2 * per_slab
    groups = slots_here // per_slab
    lat_rows = min(n_lat, 256 // width)
    block_rows = min(2 * n_orders, 64)
    lon_block = min(n_lon, 64)
    out_rows = waves * width
    dims = (n_lat_dev, n_ord_dev, n_lat, n_lon, n_orders, channels, basis_count)
    smem = pl.BlockSpec(memory_space=pltpu.SMEM)
    vmem = pl.BlockSpec(memory_space=pltpu.VMEM)
    anywhere = pl.BlockSpec(memory_space=pl.ANY)
    result = pl.pallas_call(
        functools.partial(kernel, dims),
        out_shape=jax.ShapeDtypeStruct((groups, out_rows, channels), BF16),
        in_specs=[smem, smem, vmem, anywhere, anywhere, anywhere, anywhere],
        out_specs=vmem,
        scratch_shapes=[
            pltpu.VMEM((3, n_lon, channels), BF16),
            pltpu.VMEM((3, n_lon + 2 * PAD, channels), F32),
            pltpu.VMEM((lon_block, basis_count * channels), BF16),
            pltpu.VMEM((basis_count, channels, channels), BF16),
            pltpu.VMEM((waves, channels), F32),
            pltpu.VMEM((2, channels, channels), BF16),
            pltpu.VMEM((n_lon, channels), BF16),
            pltpu.VMEM((block_rows, n_lon), BF16),
            pltpu.VMEM((n_ord_dev * groups, width, channels), BF16),
            pltpu.VMEM((groups, n_lat, width, channels), BF16),
            pltpu.VMEM((2 * out_rows, lat_rows * width), BF16),
            pltpu.SemaphoreType.DMA((4,)),
            pltpu.SemaphoreType.DMA((2,)),
            pltpu.SemaphoreType.DMA((2,)),
            pltpu.SemaphoreType.DMA((n_ord_dev,)),
            pltpu.SemaphoreType.DMA((n_ord_dev,)),
            pltpu.SemaphoreType.DMA((n_lat_dev,)),
            pltpu.SemaphoreType.DMA((n_lat_dev,)),
        ],
        compiler_params=pltpu.CompilerParams(
            collective_id=0, has_side_effects=True, vmem_limit_bytes=40 * 1024 * 1024
        ),
    )(tap_mask, tap_weight, order_slots.reshape(1, n_orders), field, basis_mix, degree_gain, spectral_mix)
    result = result.reshape(groups, waves, per_slab, 2, channels)
    return jnp.swapaxes(result, 0, 1).reshape(waves, slots_here, 2, channels)


def solution(mesh):
    in_specs = (
        P(("lat", "ord"), None, None),
        P(("lat", "ord"), None, None),
        P(("lat", "ord"), None, None),
        P(),
        P(),
        P(),
        P(),
    )
    out_specs = P("lat", "ord", None, None)
    return jax.shard_map(
        per_device, mesh=mesh, in_specs=in_specs, out_specs=out_specs, check_vma=False
    )
```

time: 37.4 us -> 26.2 us (0.70)
  Pallas kernels: 0 us -> 19.4 us
  starting transfers between devices: 14.1 us -> 0 us
  blocking collectives: 10.7 us -> 0 us
  waiting for transfers between devices: 5.66 us -> 0 us
  local copies, waits for them, and re-layouts: 4.54 us -> 6.35 us
  matrix products: 1.2 us -> 0 us
  other arithmetic: 0.49 us -> 0 us
    pallas_call x0 -> x1, Pallas kernels: none -> 19.4 us  [per_device(): pl.pallas_call(functools.partial(kernel, dims), out_shape=jax.ShapeDtypeS...]
    all_gather x1 -> x0, blocking collectives: 10.7 us -> none  [per_device(): portion = lax.all_gather(by_orders, 'lat', axis=0, tiled=True)]
    all_to_all x1 -> x0, starting transfers between devices: 9.69 us -> none  [per_device(): lax.all_to_all(fourier, 'ord', split_axis=1, concat_axis=0, tiled=True)]
    all_to_all x1 -> x0, waiting for transfers between devices: 5.66 us -> none  [per_device(): lax.all_to_all(fourier, 'ord', split_axis=1, concat_axis=0, tiled=True)]
    unnamed x13 -> x14, local copies, waits for them, and re-layouts: 0.95 us -> 5.72 us
    ppermute x2 -> x0, starting transfers between devices: 4.44 us -> none  [the longest x1 3.03 us: extended(): lax.ppermute(lax.slice_in_dim(block, block.shape[dim] - width, None, axis...]
    reshape x4 -> x0, local copies, waits for them, and re-layouts: 1.43 us -> none  [the longest x1 0.67 us: per_device(): spectra.astype(jnp.bfloat16).reshape(rows_here, n_orders, 2, channels)]
    slice x13 -> x0, local copies, waits for them, and re-layouts: 1.34 us -> none  [the longest x12 0.94 us: disco(): shifted = jnp.roll(cycle_rows, 2 - lon_step, axis=1)]
  transfers between devices with their start and end apart: 3 -> 0, of which waited for: 1 -> 0; matrix products, arithmetic and copies ran while one was open for 7% -> 0% of each run, Pallas kernels for 0% -> 0%
where the time goes in v1:
time: 26.2 us; the launch traced here: 25.8 us
  Pallas kernels  19.4 us (74%)
  local copies, waits for them, and re-layouts  6.35 us (24%)
    pallas_call x1, Pallas kernels, per_device(): pl.pallas_call(functools.partial(kernel, dims), out_shape=jax.ShapeDtypeS...  19.4 us
    unnamed x14, local copies, waits for them, and re-layouts  5.72 us
    another operation x1, local copies, waits for them, and re-layouts, per_device(): return jnp.swapaxes(result, 0, 1).reshape(waves, slots_here, 2, channels)  0.63 us

profile of v1, /device:TPU:0, one launch (start us, length us, event | category | flops | bytes accessed | tf_op | source)
XLA Modules:
  0.0 25.8 jit_solution(17475153925001465648)
XLA Ops:
  0.0 0.0 copy-start.6
  0.0 0.7 %copy-done.6 = s32[32]{0:T(128)S(1)} copy-done((s32[32]{0:T(128)S(1)}, s32[32]{0:T(128)}, u32[]{:S(2)}) %copy-start.6) | copy-done | bytes 152
  0.7 0.0 copy-start
  0.7 1.2 %copy-done = bf16[8,256,256]{2,1,0:T(8,128)(2,1)S(1)} copy-done((bf16[8,256,256]{2,1,0:T(8,128)(2,1)S(1)}, bf16[8,256,256]{2,1,0:T(8,128)(2,1)}, u32[]{:S(2)}) %copy-start) | copy-done | bytes 1048600
  1.9 0.0 copy-start.1
  1.9 0.9 %copy-done.1 = bf16[2,256,256]{2,1,0:T(8,128)(2,1)S(1)} copy-done((bf16[2,256,256]{2,1,0:T(8,128)(2,1)S(1)}, bf16[2,256,256]{2,1,0:T(8,128)(2,1)}, u32[]{:S(2)}) %copy-start.1) | copy-done | bytes 262168
  2.8 0.0 copy-start.2
  2.8 0.8 %copy-done.2 = bf16[1,64,256]{2,1,0:T(8,128)(2,1)S(1)} copy-done((bf16[1,64,256]{2,1,0:T(8,128)(2,1)S(1)}, bf16[1,64,256]{2,1,0:T(8,128)(2,1)}, u32[]{:S(2)}) %copy-start.2) | copy-done | bytes 32792
  3.6 0.0 copy-start.3
  3.6 0.8 %copy-done.3 = f32[32,256]{1,0:T(8,128)S(1)} copy-done((f32[32,256]{1,0:T(8,128)S(1)}, f32[32,256]{1,0:T(8,128)}, u32[]{:S(2)}) %copy-start.3) | copy-done | bytes 32792
  4.3 0.0 copy-start.4
  4.4 0.7 %copy-done.4 = s32[1,8,15]{2,1,0:T(8,128)S(1)} copy-done((s32[1,8,15]{2,1,0:T(8,128)S(1)}, s32[1,8,15]{2,1,0:T(8,128)}, u32[]{:S(2)}) %copy-start.4) | copy-done | bytes 504
  5.0 0.0 copy-start.5
  5.0 0.7 %copy-done.5 = f32[1,8,15]{2,1,0:T(8,128)S(1)} copy-done((f32[1,8,15]{2,1,0:T(8,128)S(1)}, f32[1,8,15]{2,1,0:T(8,128)}, u32[]{:S(2)}) %copy-start.5) | copy-done | bytes 504
  5.7 19.4 %shard_map.73 = bf16[1,64,256]{2,1,0:T(8,128)(2,1)S(1)} custom-call(s32[1,8,15]{2,1,0:T(8,128)S(1)} %copy-done.4, f32[1,8,15]{2,1,0:T(8,128)S(1)} %copy-done.5, s32[1,32]{1,0:T(1,128)S(1)} %bitcast.1, bf16[1,64,256]{2,1,0:T(8,128)(2,1)S(1)} %copy-done.2, bf16[8,256,256]{2,1,0:T(8,128)(2,1)S(1)} %copy-done, f32[32,256]{1,0:T(8,128)S(1)} %copy-done.3, ...), custom_call_target="tpu_custom_call" | custom-call | tf_op jit(solution)/shard_map/pallas_call | solution.py:312
  25.1 0.6 %reshape_transpose_reshape.3 = bf16[8,4,2,256]{3,2,1,0:T(2,128)(2,1)} reshape(bf16[1,64,256]{2,1,0:T(8,128)(2,1)S(1)} %shard_map.73) | data formatting | bytes 65536 | tf_op jit(solution)/shard_map/reshape;transpose;reshape | solution.py:342
Async XLA Ops:
  0.0 0.7 %copy-start.6 = (s32[32]{0:T(128)S(1)}, s32[32]{0:T(128)}, u32[]{:S(2)}) copy-start(s32[32]{0:T(128)} %param.11) | copy-start | bytes 388
  0.7 1.2 %copy-start = (bf16[8,256,256]{2,1,0:T(8,128)(2,1)S(1)}, bf16[8,256,256]{2,1,0:T(8,128)(2,1)}, u32[]{:S(2)}) copy-start(bf16[8,256,256]{2,1,0:T(8,128)(2,1)} %basis_hbm.1) | copy-start | bytes 3145732
  1.9 0.9 %copy-start.1 = (bf16[2,256,256]{2,1,0:T(8,128)(2,1)S(1)}, bf16[2,256,256]{2,1,0:T(8,128)(2,1)}, u32[]{:S(2)}) copy-start(bf16[2,256,256]{2,1,0:T(8,128)(2,1)} %spectral_hbm.1) | copy-start | bytes 786436
  2.8 0.8 %copy-start.2 = (bf16[1,64,256]{2,1,0:T(8,128)(2,1)S(1)}, bf16[1,64,256]{2,1,0:T(8,128)(2,1)}, u32[]{:S(2)}) copy-start(bf16[1,64,256]{2,1,0:T(8,128)(2,1)} %field_hbm.1) | copy-start | bytes 98308
  3.6 0.8 %copy-start.3 = (f32[32,256]{1,0:T(8,128)S(1)}, f32[32,256]{1,0:T(8,128)}, u32[]{:S(2)}) copy-start(f32[32,256]{1,0:T(8,128)} %gain_hbm.1) | copy-start | bytes 98308
  4.3 0.7 %copy-start.4 = (s32[1,8,15]{2,1,0:T(8,128)S(1)}, s32[1,8,15]{2,1,0:T(8,128)}, u32[]{:S(2)}) copy-start(s32[1,8,15]{2,1,0:T(8,128)} %mask_ref.1) | copy-start | bytes 1444
  5.0 0.7 %copy-start.5 = (f32[1,8,15]{2,1,0:T(8,128)S(1)}, f32[1,8,15]{2,1,0:T(8,128)}, u32[]{:S(2)}) copy-start(f32[1,8,15]{2,1,0:T(8,128)} %weight_ref.1) | copy-start | bytes 1444

commit v2 on v1

--- a/solution.py
+++ b/solution.py
@@ -44,9 +44,9 @@
 
 def kernel(
     dims,
-    mask_ref, weight_ref, slots_ref, field_hbm, basis_hbm, gain_hbm, spectral_hbm,
+    mask_hbm, weight_hbm, slots_hbm, field_hbm, basis_hbm, gain_hbm, spectral_hbm,
     out_ref,
-    rows_in, padded, taps, basis, gain, spectral, grid, table, sent, held, lat_mat,
+    mask_ref, weight_ref, slots_ref, rows_in, padded, taps, basis, gain, spectral, grid, table, sent, held, lat_mat,
     local_sem, halo_send, halo_recv, ord_send, ord_recv, lat_send, lat_recv,
 ):
     n_lat_dev, n_ord_dev, n_lat, n_lon, n_orders, channels, basis_count = dims
@@ -90,6 +90,12 @@
         gain_hbm.at[pl.ds(pl.multiple_of(lat_id * waves, waves), waves)], gain, local_sem.at[2]
     )
     spectral_copy = pltpu.make_async_copy(spectral_hbm, spectral, local_sem.at[3])
+    mask_copy = pltpu.make_async_copy(mask_hbm, mask_ref, local_sem.at[4])
+    weight_copy = pltpu.make_async_copy(weight_hbm, weight_ref, local_sem.at[5])
+    slots_copy = pltpu.make_async_copy(slots_hbm, slots_ref, local_sem.at[6])
+    slots_copy.start()
+    mask_copy.start()
+    weight_copy.start()
     own_copy.start()
     basis_copy.start()
     gain_copy.start()
@@ -103,6 +109,7 @@
     def _():
         rows_in[2] = jnp.zeros(rows_in.shape[1:], BF16)
 
+    slots_copy.wait()
     orders = slots_ref[...]
 
     def pick(slot_of_row):
@@ -172,6 +179,8 @@
     lon_block = min(n_lon, 64)
     lon_piece = 16
     basis_copy.wait()
+    mask_copy.wait()
+    weight_copy.wait()
 
     def convolve(block):
         for piece in range(lon_block // lon_piece):
@@ -306,15 +315,17 @@
     lon_block = min(n_lon, 64)
     out_rows = waves * width
     dims = (n_lat_dev, n_ord_dev, n_lat, n_lon, n_orders, channels, basis_count)
-    smem = pl.BlockSpec(memory_space=pltpu.SMEM)
     vmem = pl.BlockSpec(memory_space=pltpu.VMEM)
-    anywhere = pl.BlockSpec(memory_space=pl.ANY)
+    hbm = pl.BlockSpec(memory_space=pltpu.HBM)
     result = pl.pallas_call(
         functools.partial(kernel, dims),
         out_shape=jax.ShapeDtypeStruct((groups, out_rows, channels), BF16),
-        in_specs=[smem, smem, vmem, anywhere, anywhere, anywhere, anywhere],
+        in_specs=[hbm] * 7,
         out_specs=vmem,
         scratch_shapes=[
+            pltpu.SMEM(tap_mask.shape, jnp.int32),
+            pltpu.SMEM(tap_weight.shape, F32),
+            pltpu.VMEM((1, n_orders), jnp.int32),
             pltpu.VMEM((3, n_lon, channels), BF16),
             pltpu.VMEM((3, n_lon + 2 * PAD, channels), F32),
             pltpu.VMEM((lon_block, basis_count * channels), BF16),
@@ -326,7 +337,7 @@
             pltpu.VMEM((n_ord_dev * groups, width, channels), BF16),
             pltpu.VMEM((groups, n_lat, width, channels), BF16),
             pltpu.VMEM((2 * out_rows, lat_rows * width), BF16),
-            pltpu.SemaphoreType.DMA((4,)),
+            pltpu.SemaphoreType.DMA((7,)),
             pltpu.SemaphoreType.DMA((2,)),
             pltpu.SemaphoreType.DMA((2,)),
             pltpu.SemaphoreType.DMA((n_ord_dev,)),
@@ -335,7 +346,7 @@
             pltpu.SemaphoreType.DMA((n_lat_dev,)),
         ],
         compiler_params=pltpu.CompilerParams(
-            collective_id=0, has_side_effects=True, vmem_limit_bytes=40 * 1024 * 1024
+            collective_id=0, has_side_effects=True, vmem_limit_bytes=63 * 1024 * 1024
         ),
     )(tap_mask, tap_weight, order_slots.reshape(1, n_orders), field, basis_mix, degree_gain, spectral_mix)
     result = result.reshape(groups, waves, per_slab, 2, channels)

time: 26.2 us -> 21.2 us (0.81)
  local copies, waits for them, and re-layouts: 6.35 us -> 1.39 us
    unnamed x14 -> x0, local copies, waits for them, and re-layouts: 5.72 us -> none
    another operation x1, local copies, waits for them, and re-layouts: 0.63 us -> 1.39 us  [per_device(): return jnp.swapaxes(result, 0, 1).reshape(waves, slots_here, 2, channels)]
where the time goes in v2:
time: 21.2 us; the launch traced here: 21 us
  Pallas kernels  19.6 us (92%)
  local copies, waits for them, and re-layouts  1.39 us (7%)
    pallas_call x1, Pallas kernels, per_device(): pl.pallas_call(functools.partial(kernel, dims), out_shape=jax.ShapeDtypeS...  19.6 us
    another operation x1, local copies, waits for them, and re-layouts, per_device(): return jnp.swapaxes(result, 0, 1).reshape(waves, slots_here, 2, channels)  1.39 us

profile of v2, /device:TPU:0, one launch (start us, length us, event | category | flops | bytes accessed | tf_op | source)
XLA Modules:
  0.0 21.0 jit_solution(14894558226620068969)
XLA Ops:
  0.0 19.6 %shard_map.73 = bf16[1,64,256]{2,1,0:T(8,128)(2,1)} custom-call(s32[1,8,15]{2,1,0:T(8,128)} %mask_hbm.1, f32[1,8,15]{2,1,0:T(8,128)} %weight_hbm.1, s32[1,32]{1,0:T(1,128)} %bitcast.1, bf16[1,64,256]{2,1,0:T(8,128)(2,1)} %field_hbm.1, bf16[8,256,256]{2,1,0:T(8,128)(2,1)} %basis_hbm.1, f32[32,256]{1,0:T(8,128)} %gain_hbm.1, bf16[2,256,256]{2,1,0:T(8,128)(2,1)} %spectral_hbm.1), custom_call_target="tpu_custom_call" | custom-call | tf_op jit(solution)/shard_map/pallas_call | solution.py:320
  19.6 1.4 %reshape_transpose_reshape.3 = bf16[8,4,2,256]{3,2,1,0:T(2,128)(2,1)} reshape(bf16[1,64,256]{2,1,0:T(8,128)(2,1)} %shard_map.73) | data formatting | bytes 65536 | tf_op jit(solution)/shard_map/reshape;transpose;reshape | solution.py:353

commit v3 on v2

--- a/solution.py
+++ b/solution.py
@@ -47,7 +47,7 @@
     mask_hbm, weight_hbm, slots_hbm, field_hbm, basis_hbm, gain_hbm, spectral_hbm,
     out_ref,
     mask_ref, weight_ref, slots_ref, rows_in, padded, taps, basis, gain, spectral, grid, table, sent, held, lat_mat,
-    local_sem, halo_send, halo_recv, ord_send, ord_recv, lat_send, lat_recv,
+    local_sem, halo_send, halo_recv, all_send, all_recv, band_sem,
 ):
     n_lat_dev, n_ord_dev, n_lat, n_lon, n_orders, channels, basis_count = dims
     lat_id = lax.axis_index("lat")
@@ -60,8 +60,14 @@
     groups = slots_here // per_slab
     has_prev = row_id > 0
     has_next = row_id < n_lat - 1
-    prev_dev = ((row_id - 1) // n_ord_dev, (row_id - 1) % n_ord_dev)
-    next_dev = ((row_id + 1) // n_ord_dev, (row_id + 1) % n_ord_dev)
+    ord_mask = n_ord_dev - 1
+    at_first = (ord_id == 0).astype(jnp.int32)
+    at_last = (ord_id == ord_mask).astype(jnp.int32)
+    prev_dev = (lat_id - at_first, (ord_id + ord_mask) & ord_mask)
+    next_dev = (lat_id + at_last, (ord_id + 1) & ord_mask)
+    count = n_lat_dev * n_ord_dev
+    ord_bits = log2(n_ord_dev)
+    assert log2(count) == log2(n_lat_dev) + ord_bits
     far_prev = jnp.logical_and(ord_id == 0, has_prev)
     far_next = jnp.logical_and(ord_id == n_ord_dev - 1, has_next)
 
@@ -75,14 +81,10 @@
     def _():
         pl.semaphore_signal(barrier, inc=1, device_id=next_dev, device_id_type=MESH)
 
-    for step in range(1, n_ord_dev):
-        pl.semaphore_signal(
-            barrier, inc=1, device_id=(lat_id, lax.rem(ord_id + step, n_ord_dev)), device_id_type=MESH
-        )
+    for step in range(n_ord_dev - 1, 0, -1):
+        pl.semaphore_signal(barrier, inc=1, device_id=(lat_id, ord_id ^ step), device_id_type=MESH)
     for step in range(1, n_lat_dev):
-        pl.semaphore_signal(
-            barrier, inc=1, device_id=(lax.rem(lat_id + step, n_lat_dev), ord_id), device_id_type=MESH
-        )
+        pl.semaphore_signal(barrier, inc=1, device_id=(lat_id ^ step, ord_id), device_id_type=MESH)
 
     own_copy = pltpu.make_async_copy(field_hbm, rows_in.at[pl.ds(1, 1)], local_sem.at[0])
     basis_copy = pltpu.make_async_copy(basis_hbm, basis, local_sem.at[1])
@@ -147,8 +149,9 @@
     if single_dft:
         dft_block(0)
 
-    others = (n_ord_dev - 1) + (n_lat_dev - 1)
-    pl.semaphore_wait(barrier, others + far_prev.astype(jnp.int32) + far_next.astype(jnp.int32))
+    pl.semaphore_wait(
+        barrier, (n_ord_dev - 1) + (n_lat_dev - 1) + far_prev.astype(jnp.int32) + far_next.astype(jnp.int32)
+    )
 
     to_next = pltpu.make_async_remote_copy(
         src_ref=field_hbm, dst_ref=rows_in.at[pl.ds(0, 1)], send_sem=halo_send.at[0],
@@ -160,6 +163,8 @@
     )
     pl.when(has_next)(to_next.start)
     pl.when(has_prev)(to_prev.start)
+    for step in range(1, n_lat_dev):
+        pl.semaphore_signal(band_sem, inc=1, device_id=(lat_id ^ step, ord_id), device_id_type=MESH)
     if single_lat:
         lat_block(0, 0)
 
@@ -219,55 +224,32 @@
 
     repeat(2 * n_orders // block_rows, transform)
 
-    def ord_copy(step):
-        peer = lax.rem(ord_id + step, n_ord_dev)
-        return pltpu.make_async_remote_copy(
-            src_ref=sent.at[pl.ds(peer * groups, groups)], dst_ref=held.at[:, row_id],
-            send_sem=ord_send.at[step], recv_sem=ord_recv.at[step],
-            device_id=(lat_id, peer), device_id_type=MESH,
-        )
-
-    def ord_arrival(step):
-        source = lat_id * n_ord_dev + lax.rem(ord_id + n_ord_dev - step, n_ord_dev)
-        return pltpu.make_async_remote_copy(
-            src_ref=sent.at[pl.ds(0, groups)], dst_ref=held.at[:, source],
-            send_sem=ord_send.at[step], recv_sem=ord_recv.at[step],
-            device_id=(lat_id, ord_id), device_id_type=MESH,
-        )
-
-    for step in range(1, n_ord_dev):
-        ord_copy(step).start()
+    def send(step):
+        lat_step, ord_step = step >> ord_bits, step & ord_mask
+        target = (lat_id ^ lat_step, ord_id ^ ord_step)
+        pltpu.make_async_remote_copy(
+            src_ref=sent.at[pl.ds(target[1] * groups, groups)], dst_ref=held.at[:, row_id],
+            send_sem=all_send.at[0], recv_sem=all_recv.at[0],
+            device_id=target, device_id_type=MESH,
+        ).start()
+
+    pl.semaphore_wait(band_sem, n_lat_dev - 1)
+    if count <= 64:
+        for step in sorted(range(1, count), key=lambda step: (-(step & ord_mask), -step)):
+            send(step)
+    else:
+        pl.loop(1, count)(send)
     held[:, row_id] = sent[pl.ds(ord_id * groups, groups)]
-    for step in range(1, n_ord_dev):
-        ord_arrival(step).wait_recv()
-
-    def lat_copy(step):
-        band = pl.ds(lat_id * n_ord_dev, n_ord_dev)
-        return pltpu.make_async_remote_copy(
-            src_ref=held.at[:, band], dst_ref=held.at[:, band],
-            send_sem=lat_send.at[step], recv_sem=lat_recv.at[step],
-            device_id=(lax.rem(lat_id + step, n_lat_dev), ord_id), device_id_type=MESH,
-        )
-
-    def lat_arrival(step):
-        source = lax.rem(lat_id + n_lat_dev - step, n_lat_dev)
-        band = pl.ds(source * n_ord_dev, n_ord_dev)
-        return pltpu.make_async_remote_copy(
-            src_ref=held.at[:, band], dst_ref=held.at[:, band],
-            send_sem=lat_send.at[step], recv_sem=lat_recv.at[step],
-            device_id=(lat_id, ord_id), device_id_type=MESH,
-        )
-
-    for step in range(1, n_lat_dev):
-        lat_copy(step).start()
     pl.when(has_next)(to_next.wait_send)
     pl.when(has_prev)(to_prev.wait_send)
-    for step in range(1, n_ord_dev):
-        ord_copy(step).wait_send()
     gain_copy.wait()
     spectral_copy.wait()
-    for step in range(1, n_lat_dev):
-        lat_arrival(step).wait_recv()
+    arrivals = pltpu.make_async_remote_copy(
+        src_ref=held.at[:, pl.ds(0, count - 1)], dst_ref=held.at[:, pl.ds(0, count - 1)],
+        send_sem=all_send.at[0], recv_sem=all_recv.at[0],
+        device_id=(lat_id, ord_id ^ 1), device_id_type=MESH,
+    )
+    arrivals.wait_recv()
 
     def latitude(group, part):
         rows = held[group, pl.ds(part * lat_rows, lat_rows)].reshape(lat_rows * width, channels)
@@ -293,8 +275,7 @@
         out_ref[group] = result.astype(BF16)
 
     repeat(groups, finish)
-    for step in range(1, n_lat_dev):
-        lat_copy(step).wait_send()
+    arrivals.wait_send()
 
 
 def per_device(field, tap_mask, tap_weight, basis_mix, order_slots, degree_gain, spectral_mix):
@@ -340,10 +321,9 @@
             pltpu.SemaphoreType.DMA((7,)),
             pltpu.SemaphoreType.DMA((2,)),
             pltpu.SemaphoreType.DMA((2,)),
-            pltpu.SemaphoreType.DMA((n_ord_dev,)),
-            pltpu.SemaphoreType.DMA((n_ord_dev,)),
-            pltpu.SemaphoreType.DMA((n_lat_dev,)),
-            pltpu.SemaphoreType.DMA((n_lat_dev,)),
+            pltpu.SemaphoreType.DMA((1,)),
+            pltpu.SemaphoreType.DMA((1,)),
+            pltpu.SemaphoreType.REGULAR,
         ],
         compiler_params=pltpu.CompilerParams(
             collective_id=0, has_side_effects=True, vmem_limit_bytes=63 * 1024 * 1024

time: 21.2 us -> 18.1 us (0.85)
  Pallas kernels: 19.6 us -> 16.5 us
    pallas_call x1, Pallas kernels: 19.6 us -> 16.5 us  [per_device(): pl.pallas_call(functools.partial(kernel, dims), out_shape=jax.ShapeDtypeS...]
where the time goes in v3:
time: 18.1 us; the launch traced here: 17.9 us
  Pallas kernels  16.5 us (91%)
  local copies, waits for them, and re-layouts  1.39 us (8%)
    pallas_call x1, Pallas kernels, per_device(): pl.pallas_call(functools.partial(kernel, dims), out_shape=jax.ShapeDtypeS...  16.5 us
    another operation x1, local copies, waits for them, and re-layouts, per_device(): return jnp.swapaxes(result, 0, 1).reshape(waves, slots_here, 2, channels)  1.39 us

profile of v3, /device:TPU:0, one launch (start us, length us, event | category | flops | bytes accessed | tf_op | source)
XLA Modules:
  0.0 17.9 jit_solution(1537683375899478662)
XLA Ops:
  0.0 16.5 %shard_map.73 = bf16[1,64,256]{2,1,0:T(8,128)(2,1)} custom-call(s32[1,8,15]{2,1,0:T(8,128)} %mask_hbm.1, f32[1,8,15]{2,1,0:T(8,128)} %weight_hbm.1, s32[1,32]{1,0:T(1,128)} %bitcast.1, bf16[1,64,256]{2,1,0:T(8,128)(2,1)} %field_hbm.1, bf16[8,256,256]{2,1,0:T(8,128)(2,1)} %basis_hbm.1, f32[32,256]{1,0:T(8,128)} %gain_hbm.1, bf16[2,256,256]{2,1,0:T(8,128)(2,1)} %spectral_hbm.1), custom_call_target="tpu_custom_call" | custom-call | tf_op jit(solution)/shard_map/pallas_call | solution.py:301
  16.5 1.4 %reshape_transpose_reshape.3 = bf16[8,4,2,256]{3,2,1,0:T(2,128)(2,1)} reshape(bf16[1,64,256]{2,1,0:T(8,128)(2,1)} %shard_map.73) | data formatting | bytes 65536 | tf_op jit(solution)/shard_map/reshape;transpose;reshape | solution.py:333

commit v4 on v3

--- a/solution.py
+++ b/solution.py
@@ -46,7 +46,7 @@
     dims,
     mask_hbm, weight_hbm, slots_hbm, field_hbm, basis_hbm, gain_hbm, spectral_hbm,
     out_ref,
-    mask_ref, weight_ref, slots_ref, rows_in, padded, taps, basis, gain, spectral, grid, table, sent, held, lat_mat,
+    mask_ref, weight_ref, slots_ref, rows_in, padded, partial, taps, basis, gain, spectral, grid, table, sent, held, lat_mat,
     local_sem, halo_send, halo_recv, all_send, all_recv, band_sem,
 ):
     n_lat_dev, n_ord_dev, n_lat, n_lon, n_orders, channels, basis_count = dims
@@ -149,16 +149,17 @@
     if single_dft:
         dft_block(0)
 
+    own_copy.wait()
     pl.semaphore_wait(
         barrier, (n_ord_dev - 1) + (n_lat_dev - 1) + far_prev.astype(jnp.int32) + far_next.astype(jnp.int32)
     )
 
     to_next = pltpu.make_async_remote_copy(
-        src_ref=field_hbm, dst_ref=rows_in.at[pl.ds(0, 1)], send_sem=halo_send.at[0],
+        src_ref=rows_in.at[pl.ds(1, 1)], dst_ref=rows_in.at[pl.ds(0, 1)], send_sem=halo_send.at[0],
         recv_sem=halo_recv.at[0], device_id=next_dev, device_id_type=MESH,
     )
     to_prev = pltpu.make_async_remote_copy(
-        src_ref=field_hbm, dst_ref=rows_in.at[pl.ds(2, 1)], send_sem=halo_send.at[1],
+        src_ref=rows_in.at[pl.ds(1, 1)], dst_ref=rows_in.at[pl.ds(2, 1)], send_sem=halo_send.at[1],
         recv_sem=halo_recv.at[1], device_id=prev_dev, device_id_type=MESH,
     )
     pl.when(has_next)(to_next.start)
@@ -174,44 +175,52 @@
         padded[which, pl.ds(0, PAD)] = row[n_lon - PAD:]
         padded[which, pl.ds(PAD + n_lon, PAD)] = row[:PAD]
 
-    own_copy.wait()
-    spread(1)
-    pl.when(has_prev)(to_next.wait_recv)
-    spread(0)
-    pl.when(has_next)(to_prev.wait_recv)
-    spread(2)
-
     lon_block = min(n_lon, 64)
     lon_piece = 16
-    basis_copy.wait()
-    mask_copy.wait()
-    weight_copy.wait()
+
+    def tap_terms(lat_steps, block, piece, b, total):
+        first = block * lon_block + piece * lon_piece
+        for lat_step in lat_steps:
+            if isinstance(block, int):
+                window = padded[lat_step, first: first + lon_piece + 2 * PAD]
+            else:
+                window = padded[lat_step, pl.ds(pl.multiple_of(first, lon_piece), lon_piece + 2 * PAD)]
+            for lon_step in range(5):
+                tap = 5 * lat_step + lon_step
+                shifted = window[PAD + lon_step - 2: PAD + lon_step - 2 + lon_piece]
+                term = (mask_ref[0, b, tap].astype(F32) * weight_ref[0, b, tap]) * shifted
+                total = term if total is None else total + term
+        return total
+
+    def place(block, piece):
+        first = block * lon_block + piece * lon_piece
+        return pl.ds(first if isinstance(block, int) else pl.multiple_of(first, lon_piece), lon_piece)
+
+    def middle(block):
+        for piece in range(lon_block // lon_piece):
+            for b in range(basis_count):
+                partial[b, place(block, piece)] = tap_terms((1,), block, piece, b, None)
 
     def convolve(block):
         for piece in range(lon_block // lon_piece):
-            offset = piece * lon_piece
-            first = offset if isinstance(block, int) else pl.multiple_of(block * lon_block, lon_block) + offset
-            if isinstance(block, int):
-                window = padded[:, first: first + lon_piece + 2 * PAD]
-            else:
-                window = padded[:, pl.ds(first, lon_piece + 2 * PAD)]
-            shifted = [
-                window[lat_step, PAD + lon_step - 2: PAD + lon_step - 2 + lon_piece]
-                for lat_step in range(3)
-                for lon_step in range(5)
-            ]
             for b in range(basis_count):
-                total = None
-                for tap in range(15):
-                    term = (mask_ref[0, b, tap].astype(F32) * weight_ref[0, b, tap]) * shifted[tap]
-                    total = term if total is None else total + term
-                taps[pl.ds(offset, lon_piece), pl.ds(b * channels, channels)] = total.astype(BF16)
+                total = tap_terms((0, 2), block, piece, b, partial[b, place(block, piece)])
+                taps[pl.ds(piece * lon_piece, lon_piece), pl.ds(b * channels, channels)] = total.astype(BF16)
         mixed = jnp.dot(
             taps[...], basis[...].reshape(basis_count * channels, channels), preferred_element_type=F32
         )
         start = block * lon_block if isinstance(block, int) else pl.multiple_of(block * lon_block, lon_block)
         grid[pl.ds(start, lon_block)] = mixed.astype(BF16)
 
+    spread(1)
+    mask_copy.wait()
+    weight_copy.wait()
+    repeat(n_lon // lon_block, middle)
+    basis_copy.wait()
+    pl.when(has_prev)(to_next.wait_recv)
+    spread(0)
+    pl.when(has_next)(to_prev.wait_recv)
+    spread(2)
     repeat(n_lon // lon_block, convolve)
 
     slabs = block_rows // width
@@ -300,7 +309,7 @@
     hbm = pl.BlockSpec(memory_space=pltpu.HBM)
     result = pl.pallas_call(
         functools.partial(kernel, dims),
-        out_shape=jax.ShapeDtypeStruct((groups, out_rows, channels), BF16),
+        out_shape=pltpu.VMEM((groups, out_rows, channels), BF16),
         in_specs=[hbm] * 7,
         out_specs=vmem,
         scratch_shapes=[
@@ -309,6 +318,7 @@
             pltpu.VMEM((1, n_orders), jnp.int32),
             pltpu.VMEM((3, n_lon, channels), BF16),
             pltpu.VMEM((3, n_lon + 2 * PAD, channels), F32),
+            pltpu.VMEM((basis_count, n_lon, channels), F32),
             pltpu.VMEM((lon_block, basis_count * channels), BF16),
             pltpu.VMEM((basis_count, channels, channels), BF16),
             pltpu.VMEM((waves, channels), F32),
@@ -328,7 +338,7 @@
         compiler_params=pltpu.CompilerParams(
             collective_id=0, has_side_effects=True, vmem_limit_bytes=63 * 1024 * 1024
         ),
-    )(tap_mask, tap_weight, order_slots.reshape(1, n_orders), field, basis_mix, degree_gain, spectral_mix)
+    )(*[pltpu.with_memory_space_constraint(x, pltpu.HBM) for x in (tap_mask, tap_weight, order_slots.reshape(1, n_orders), field, basis_mix, degree_gain, spectral_mix)])
     result = result.reshape(groups, waves, per_slab, 2, channels)
     return jnp.swapaxes(result, 0, 1).reshape(waves, slots_here, 2, channels)
 

time: 18.1 us -> 16 us (0.88)
  Pallas kernels: 16.5 us -> 15.2 us
  local copies, waits for them, and re-layouts: 1.39 us -> 0.63 us
    pallas_call x1, Pallas kernels: 16.5 us -> 15.2 us  [per_device(): pl.pallas_call(functools.partial(kernel, dims), out_shape=pltpu.VMEM((gro...]
    another operation x1, local copies, waits for them, and re-layouts: 1.39 us -> 0.63 us  [per_device(): return jnp.swapaxes(result, 0, 1).reshape(waves, slots_here, 2, channels)]
where the time goes in v4:
time: 16 us; the launch traced here: 15.9 us
  Pallas kernels  15.2 us (95%)
  local copies, waits for them, and re-layouts  0.63 us (4%)
    pallas_call x1, Pallas kernels, per_device(): pl.pallas_call(functools.partial(kernel, dims), out_shape=pltpu.VMEM((gro...  15.2 us
    another operation x1, local copies, waits for them, and re-layouts, per_device(): return jnp.swapaxes(result, 0, 1).reshape(waves, slots_here, 2, channels)  0.63 us

profile of v4, /device:TPU:0, one launch (start us, length us, event | category | flops | bytes accessed | tf_op | source)
XLA Modules:
  0.0 15.9 jit_solution(3026934590300383133)
XLA Ops:
  0.0 15.2 %shard_map.73 = bf16[1,64,256]{2,1,0:T(8,128)(2,1)S(1)} custom-call(s32[1,8,15]{2,1,0:T(8,128)} %mask_hbm.1, f32[1,8,15]{2,1,0:T(8,128)} %weight_hbm.1, s32[1,32]{1,0:T(1,128)} %bitcast.1, bf16[1,64,256]{2,1,0:T(8,128)(2,1)} %field_hbm.1, bf16[8,256,256]{2,1,0:T(8,128)(2,1)} %basis_hbm.1, f32[32,256]{1,0:T(8,128)} %gain_hbm.1, bf16[2,256,256]{2,1,0:T(8,128)(2,1)} %spectral_hbm.1), custom_call_target="tpu_custom_call" | custom-call | tf_op jit(solution)/shard_map/pallas_call | solution.py:310
  15.2 0.6 %reshape_transpose_reshape.3 = bf16[8,4,2,256]{3,2,1,0:T(2,128)(2,1)} reshape(bf16[1,64,256]{2,1,0:T(8,128)(2,1)S(1)} %shard_map.73) | data formatting | bytes 65536 | tf_op jit(solution)/shard_map/reshape;transpose;reshape | solution.py:343
